TPU v7x, 32 devices: a whole 2x2x4 slice. The times are simulated.
32 devices in a mesh: scene: 4 (over y, x), region: 8 (over z, core).
Axes of the slice: x: 2, y: 2, z: 4, core: 2. Of those that a mesh axis runs over, the one named last changes fastest.
Arguments:
- features: bfloat16 [4, 8, 1728, 128], P('scene', 'region'), may hold values from -6 to 6
- voxel_mask: int32 [4, 8, 1728], P('scene', 'region'), may hold values 0 or 1
- cotangent: bfloat16 [4, 8, 1728, 128], P('scene', 'region'), may hold values from -6 to 6
- norm_gain: float32 [128], replicated, may hold values from 0.1 to 1.9
- conv_weight: bfloat16 [27, 128, 128], replicated, may hold values from -0.109375 to 0.109375
- block_owner: int32 [4, 8], P('scene'), may hold values from 0 to 7, each once within a row
Outputs:
- block_output: bfloat16 [4, 8, 1728, 128], P('scene', 'region')
- input_grad: bfloat16 [4, 8, 1728, 128], P('scene', 'region')
- weight_update: float32 [3456, 128], P('region')
Inputs may be any that keep to these rules, and one draw needn't show every extreme that they name: `block_owner`: each row names every slot of the scene exactly once.
All inputs are finite; a program needn't handle non-finite values. No bound on the sum of `voxel_mask` on one device may be relied on, other than what follows from the above.
Results may differ from a plain program's by a relative error of at most 0.0029.
Values may be sent and summed in bfloat16 or wider, within the bound.
A program may use at most 128 MiB of HBM per device.

v0:
```python
import math

import jax
import jax.numpy as jnp
import numpy as np
from jax import lax
from jax.sharding import PartitionSpec as P

BS = 12
TAPS = 27
GY = 4
GZ = 2


NORM_EPSILON = 1e-06
OFFSETS = [(a, b, c) for a in (-1, 0, 1) for b in (-1, 0, 1) for c in (-1, 0, 1)]
DIRECTIONS = [
    item
    for level in (1, 2, 3)
    for item in OFFSETS
    if abs(item[0]) + abs(item[1]) + abs(item[2]) == level
]
COLUMNS = [(a, b) for a in (-1, 0, 1) for b in (-1, 0, 1)]


def side_range(component, edge):
    if component == 1:
        return (edge - 1, edge)
    if component == -1:
        return (0, 1)
    return (0, edge)


def halo_range(component, edge):
    if component == 1:
        return (edge + 1, edge + 2)
    if component == -1:
        return (0, 1)
    return (1, edge + 1)


def slab_count(direction, edge):
    total = 1
    for component in direction:
        total = total * (1 if component != 0 else edge)
    return total


def row_directions(edge, region_count):
    labels = []
    for position, direction in enumerate(DIRECTIONS):
        labels = labels + [position] * slab_count(direction, edge)
    per_peer = -(-len(labels) // region_count)
    labels = labels + [len(DIRECTIONS)] * (per_peer * region_count - len(labels))
    return (np.array(labels, dtype=np.int32).reshape(per_peer, region_count), len(labels), per_peer)


def holder_table(owner_row, region_count):
    slot_ids = jnp.arange(region_count, dtype=jnp.int32)
    block_of = jnp.sum(
        jnp.where(owner_row[None, :] == slot_ids[:, None], slot_ids[None, :], 0), axis=1
    )
    layer = GY * GZ
    across = region_count // layer
    block_x = block_of // layer
    block_y = block_of // GZ % GY
    block_z = block_of % GZ
    columns = []
    for direction in DIRECTIONS:
        near_x = block_x + direction[0]
        near_y = block_y + direction[1]
        near_z = block_z + direction[2]
        inside = (
            (near_x >= 0)
            & (near_x < across)
            & (near_y >= 0)
            & (near_y < GY)
            & (near_z >= 0)
            & (near_z < GZ)
        )
        target = jnp.clip(near_x * layer + near_y * GZ + near_z, 0, region_count - 1)
        holder = jnp.take(owner_row, target, axis=0)
        columns.append(jnp.where(inside, holder, -1))
    columns.append(jnp.full((region_count,), -1, jnp.int32))
    return jnp.stack(columns, axis=1)


def route_plan(owner_row, region_count):
    labels, padded_rows, per_peer = row_directions(BS, region_count)
    myself = lax.axis_index("region")
    labels_now = lax.dynamic_index_in_dim(jnp.asarray(labels), myself, 1, keepdims=False)
    holders = holder_table(owner_row, region_count)
    sources = jnp.take(holders, labels_now, axis=1)
    valid = sources >= 0
    positions = jnp.arange(per_peer, dtype=jnp.int32)[None, :]
    source_rows = jnp.where(valid, sources * per_peer + positions, 0).reshape(-1)
    return (source_rows, valid.astype(jnp.bfloat16), per_peer)


def dealt_shell(cube, region_count, per_peer):
    edge = cube.shape[0]
    width = cube.shape[3]
    pieces = []
    for direction in DIRECTIONS:
        spans = [side_range(-component, edge) for component in direction]
        pieces.append(
            cube[
                spans[0][0] : spans[0][1], spans[1][0] : spans[1][1], spans[2][0] : spans[2][1]
            ].reshape(-1, width)
        )
    rows = jnp.concatenate(pieces, axis=0)
    rows = jnp.pad(rows, ((0, per_peer * region_count - rows.shape[0]), (0, 0)))
    return rows.reshape(per_peer, region_count, width).transpose(1, 0, 2)


def pick_rows(holdings, plan):
    source_rows, valid, per_peer = plan
    width = holdings.shape[2]
    flat = holdings.reshape(-1, width)
    picked = jnp.take(flat, source_rows, axis=0).reshape(holdings.shape[0], per_peer, width)
    return picked * valid[..., None]


def relay(plan, cube, region_count):
    dealt = lax.all_to_all(
        dealt_shell(cube, region_count, plan[2]), "region", split_axis=0, concat_axis=0, tiled=True
    )
    return lax.all_to_all(pick_rows(dealt, plan), "region", split_axis=0, concat_axis=0, tiled=True)


def assemble(received, cube):
    edge = cube.shape[0]
    width = cube.shape[3]
    whole = received.transpose(1, 0, 2).reshape(-1, width)
    padded = jnp.pad(cube, ((1, 1), (1, 1), (1, 1), (0, 0)))
    offset = 0
    for direction in DIRECTIONS:
        spans = [halo_range(component, edge) for component in direction]
        lengths = [upper - lower for lower, upper in spans]
        count = lengths[0] * lengths[1] * lengths[2]
        piece = whole[offset : offset + count].reshape(lengths[0], lengths[1], lengths[2], width)
        padded = padded.at[
            spans[0][0] : spans[0][1], spans[1][0] : spans[1][1], spans[2][0] : spans[2][1]
        ].set(piece)
        offset = offset + count
    return padded


def column_window(padded, shift_x, shift_y, edge, width):
    column = padded[1 + shift_x : 1 + shift_x + edge, 1 + shift_y : 1 + shift_y + edge]
    return jnp.concatenate(
        [column[:, :, 1 + shift_z : 1 + shift_z + edge] for shift_z in (-1, 0, 1)], axis=-1
    ).reshape(-1, 3 * width)


def convolve(padded_act, padded_grad, grad_block, conv_weight):
    edge = padded_act.shape[0] - 2
    width = padded_act.shape[3]
    forward = jnp.zeros((edge * edge * edge, width), jnp.float32)
    backward = jnp.zeros((edge * edge * edge, width), jnp.float32)
    terms = []
    for group_index, (shift_x, shift_y) in enumerate(COLUMNS):
        group_weight = conv_weight[3 * group_index : 3 * group_index + 3]
        window = column_window(padded_act, shift_x, shift_y, edge, width)
        forward = forward + jnp.dot(
            window, group_weight.reshape(3 * width, width), preferred_element_type=jnp.float32
        )
        mirror_column = padded_grad[
            1 - shift_x : 1 - shift_x + edge, 1 - shift_y : 1 - shift_y + edge
        ]
        mirror = jnp.concatenate(
            [mirror_column[:, :, 1 - shift_z : 1 - shift_z + edge] for shift_z in (-1, 0, 1)],
            axis=-1,
        ).reshape(-1, 3 * width)
        backward = backward + jnp.dot(
            mirror,
            group_weight.transpose(0, 2, 1).reshape(3 * width, width),
            preferred_element_type=jnp.float32,
        )
        terms.append(
            lax.dot_general(
                window, grad_block, (((0,), (0,)), ((), ())), preferred_element_type=jnp.float32
            )
        )
    return (forward, backward, jnp.concatenate(terms, axis=0).reshape(TAPS, width, width))


def body(features, voxel_mask, cotangent, norm_gain, conv_weight, block_owner):
    width = features.shape[-1]
    region_count = lax.axis_size("region")
    plan = route_plan(block_owner[0], region_count)
    inputs = features[0, 0].astype(jnp.float32)
    mask_col = voxel_mask[0, 0].astype(jnp.float32)[:, None]
    rinv = lax.rsqrt(jnp.mean(inputs * inputs, axis=-1, keepdims=True) + NORM_EPSILON)
    normed = inputs * rinv
    pre = normed * norm_gain
    activity = (jax.nn.silu(pre) * mask_col).astype(jnp.bfloat16)
    grad_out = cotangent[0, 0] * voxel_mask[0, 0].astype(jnp.bfloat16)[:, None]
    act_cube = activity.reshape(BS, BS, BS, width)
    grad_cube = grad_out.reshape(BS, BS, BS, width)
    act_recv = relay(plan, act_cube, region_count)
    grad_recv = relay(plan, grad_cube, region_count)
    padded_act = assemble(act_recv, act_cube)
    padded_grad = assemble(grad_recv, grad_cube)
    forward, backward, weight_grad = convolve(padded_act, padded_grad, grad_out, conv_weight)
    block_output = (inputs + forward * mask_col).astype(jnp.bfloat16)
    slope = jax.nn.sigmoid(pre)
    dnorm = backward * mask_col * (slope * (1.0 + pre * (1.0 - slope))) * norm_gain
    dinput = rinv * (dnorm - normed * jnp.mean(dnorm * normed, axis=-1, keepdims=True))
    input_grad = (cotangent[0, 0].astype(jnp.float32) + dinput).astype(jnp.bfloat16)
    flat_grad = weight_grad.reshape(-1, width)
    share_rows = flat_grad.shape[0] // region_count
    limit = math.sqrt(flat_grad.shape[0] * width)
    summed = lax.psum(flat_grad, "region")
    total_squares = jnp.sum(summed * summed)
    share = lax.dynamic_slice_in_dim(summed, lax.axis_index("region") * share_rows, share_rows, 0)
    factor = jnp.minimum(1.0, limit / jnp.sqrt(total_squares))
    update = lax.psum(share * factor, "scene") / lax.axis_size("scene")
    return (block_output.reshape(features.shape), input_grad.reshape(cotangent.shape), update)


def solution(mesh):
    in_specs = (
        P("scene", "region", None, None),
        P("scene", "region", None),
        P("scene", "region", None, None),
        P(),
        P(),
        P("scene", None),
    )
    out_specs = (
        P("scene", "region", None, None),
        P("scene", "region", None, None),
        P("region", None),
    )
    return jax.shard_map(body, mesh=mesh, in_specs=in_specs, out_specs=out_specs, check_vma=False)
```

profile of v0, /device:TPU:0, one launch (start us, length us, event | category | flops | bytes accessed | tf_op | source)
XLA Modules:
  0.0 337.5 jit_solution(2052166932795529801)
XLA Ops:
  13.1 6.3 %all-to-all-start.2 = ((bf16[8,127,128]{2,1,0:T(8,128)(2,1)}), bf16[8,127,128]{2,1,0:T(8,128)(2,1)S(1)}, u32[]{:S(2)}, u32[]{:S(2)}) async-start(bf16[8,127,128]{2,1,0:T(8,128)(2,1)} %bitcast.363), calls=%async_computation.2 | async-start | bytes 524288 | tf_op jit(solution)/shard_map/all_to_all | solution.py:125
  45.5 2.4 slice_bitcast_fusion.64
  48.1 3.3 gather_fusion.28
  52.7 5.1 %all-to-all-start.3 = ((bf16[8,127,128]{2,1,0:T(8,128)(2,1)}), bf16[8,127,128]{2,1,0:T(8,128)(2,1)S(1)}, u32[]{:S(2)}, u32[]{:S(2)}) async-start(bf16[8,127,128]{2,1,0:T(8,128)(2,1)} %broadcast_multiply_fusion.2), calls=%async_computation.3 | async-start | bytes 524288 | tf_op jit(solution)/shard_map/all_to_all | solution.py:128
  64.0 1.6 copy.290
  73.3 1.5 scatter.220
  74.8 1.5 scatter.221
  78.2 2.2 fusion.65
  80.4 4.9 %fusion.64 = (bf16[12,12,12,128]{3,2,1,0:T(8,128)(2,1)}, bf16[12,12,12,128]{3,2,1,0:T(8,128)(2,1)}, bf16[12,12,12,128]{3,2,1,0:T(8,128)(2,1)}, bf16[12,12,12,128...) fusion(bf16[14,14,14,128]{3,2,1,0:T(8,128)(2,1)S(1)} %scatter.259), kind=kLoop, calls=%fused_computation.406 | loop fusion | bytes 16809984 | tf_op jit(solution)/shard_map/slice | solution.py:172
  86.9 1.8 pad_maximum_fusion.9
  89.0 1.8 pad_maximum_fusion.17
  92.0 1.8 pad_maximum_fusion.11
  95.0 1.8 pad_maximum_fusion.16
  98.1 1.8 pad_maximum_fusion.15
  101.1 1.8 pad_maximum_fusion.14
  104.1 1.8 pad_maximum_fusion.13
  107.2 1.8 pad_maximum_fusion.12
  119.9 1.9 fusion.8
  122.9 23.5 %all_to_all.20 = bf16[8,127,128]{2,1,0:T(8,128)(2,1)S(1)} all-to-all(bf16[8,127,128]{2,1,0:T(8,128)(2,1)S(1)} %bitcast.398), channel_id=1, replica_groups=mesh['scene'=4,'region'=8] {'region'}, dimensions={0} | all-to-all | bytes 520192 | tf_op jit(solution)/shard_map/all_to_all | solution.py:125
  146.6 3.3 gather_fusion.27
  151.2 3.4 %all-to-all-start.1 = ((bf16[8,127,128]{2,1,0:T(8,128)(2,1)}), bf16[8,127,128]{2,1,0:T(8,128)(2,1)S(1)}, u32[]{:S(2)}, u32[]{:S(2)}) async-start(bf16[8,127,128]{2,1,0:T(8,128)(2,1)} %broadcast_multiply_fusion.3), calls=%async_computation.1 | async-start | bytes 524288 | tf_op jit(solution)/shard_map/all_to_all | solution.py:128
  154.9 9.4 %all-to-all-done.1 = bf16[8,127,128]{2,1,0:T(8,128)(2,1)S(1)} async-done(((bf16[8,127,128]{2,1,0:T(8,128)(2,1)}), bf16[8,127,128]{2,1,0:T(8,128)(2,1)S(1)}, u32[]{:S(2)}, u32[]{:S(2)}) %all-to-all-start.1) | async-done | bytes 260128 | tf_op jit(solution)/shard_map/all_to_all | solution.py:128
  165.3 1.5 scatter.176
  166.9 1.5 scatter.179
  170.2 2.2 fusion.67
  172.3 4.7 %fusion.66 = (bf16[12,12,12,128]{3,2,1,0:T(8,128)(2,1)}, bf16[12,12,12,128]{3,2,1,0:T(8,128)(2,1)}, bf16[12,12,12,128]{3,2,1,0:T(8,128)(2,1)}, bf16[12,12,12,128...) fusion(bf16[14,14,14,128]{3,2,1,0:T(8,128)(2,1)S(1)} %scatter.215), kind=kLoop, calls=%fused_computation.408 | loop fusion | bytes 16809984 | tf_op jit(solution)/shard_map/slice | solution.py:152
  178.7 1.8 pad_maximum_fusion
  181.1 2.7 convolution_dynamic-update-slice_fusion.8
  186.0 1.8 pad_maximum_fusion.2
  189.1 1.8 pad_maximum_fusion.7
  192.1 1.8 pad_maximum_fusion.6
  195.1 1.8 pad_maximum_fusion.5
  198.1 1.8 pad_maximum_fusion.4
  201.1 1.8 pad_maximum_fusion.3
  204.4 3.2 convolution_dynamic-update-slice_fusion.7
  207.5 2.7 convolution_dynamic-update-slice_fusion.6
  210.2 1.6 convolution_dynamic-update-slice_fusion.5
  211.8 1.6 convolution_dynamic-update-slice_fusion.4
  213.4 1.6 convolution_dynamic-update-slice_fusion.3
  215.0 1.6 convolution_dynamic-update-slice_fusion.2
  216.6 1.6 convolution_dynamic-update-slice_fusion.1
  218.1 1.6 convolution_dynamic-update-slice_fusion
  219.8 1.8 convolution_add_fusion.15
  227.3 54.4 %all-reduce.5.cloned.1.call-done = f32[3456,128]{1,0:T(8,128)} async-done(((f32[3456,128]{1,0:T(8,128)}), f32[3456,128]{1,0:T(8,128)}) %all-reduce.5.cloned.1.call-update) | async-done | bytes 1769488 | tf_op jit(solution)/shard_map/psum | solution.py:214
  281.7 2.5 multiply_reduce_fusion
  284.9 1.6 dynamic-slice_multiply_fusion
  287.8 40.9 %all-reduce.7.cloned.1.call-done = f32[432,128]{1,0:T(8,128)} async-done(((f32[432,128]{1,0:T(8,128)}), f32[432,128]{1,0:T(8,128)}) %all-reduce.7.cloned.1.call-update) | async-done | bytes 221200 | tf_op jit(solution)/shard_map/psum | solution.py:218
  328.8 1.6 broadcast_multiply_fusion.4
  (450 shorter events, 92.5 us)
Async XLA Ops:
  10.5 10.4 %copy-start.62 = (s32[1,1,1728]{2,1,0:T(1,128)S(1)}, s32[1,1,1728]{2,1,0:T(1,128)}, u32[]{:S(2)}) copy-start(s32[1,1,1728]{2,1,0:T(1,128)} %param.116) | copy-start | bytes 20740
  10.5 10.4 %copy-start = (s32[1,8]{1,0:T(1,128)S(1)}, s32[1,8]{1,0:T(1,128)}, u32[]{:S(2)}) copy-start(s32[1,8]{1,0:T(1,128)} %param.120) | copy-start | bytes 100
  13.1 34.8 %all-to-all-start.2 = ((bf16[8,127,128]{2,1,0:T(8,128)(2,1)}), bf16[8,127,128]{2,1,0:T(8,128)(2,1)S(1)}, u32[]{:S(2)}, u32[]{:S(2)}) async-start(bf16[8,127,128]{2,1,0:T(8,128)(2,1)} %bitcast.363), calls=%async_computation.2 | async-start | bytes 524288 | tf_op jit(solution)/shard_map/all_to_all | solution.py:125
  20.9 19.4 %copy-start.53 = (f32[1728]{0:T(1024)}, f32[1728]{0:T(1024)S(1)}, u32[]{:S(2)}) copy-start(f32[1728]{0:T(1024)S(1)} %convert_reduce_fusion.1) | copy-start | bytes 20740
  34.2 5.4 %copy-start.1 = (bf16[1,1,1728,128]{3,2,1,0:T(8,128)(2,1)S(1)}, bf16[1,1,1728,128]{3,2,1,0:T(8,128)(2,1)}, u32[]{:S(2)}) copy-start(bf16[1,1,1728,128]{3,2,1,0:T(8,128)(2,1)} %param.115) | copy-start | bytes 1327108
  36.9 3.9 %copy-start.78 = (f32[128]{0:T(128)S(1)}, f32[128]{0:T(128)}, u32[]{:S(2)}) copy-start(f32[128]{0:T(128)} %param.118) | copy-start | bytes 1540
  41.6 30.0 %copy-start.24 = (bf16[12,12,12,128]{3,2,1,0:T(8,128)(2,1)}, bf16[12,12,12,128]{3,2,1,0:T(8,128)(2,1)S(1)}, u32[]{:S(2)}) copy-start(bf16[12,12,12,128]{3,2,1,0:T(8,128)(2,1)S(1)} %multiply_convert_fusion) | copy-start | bytes 1327108
  43.7 7.7 %copy-start.58 = (s32[1024]{0:T(1024)}, s32[1024]{0:T(1024)S(1)}, u32[]{:S(2)}) copy-start(s32[1024]{0:T(1024)S(1)} %pad_clamp_fusion) | copy-start | bytes 12292
  45.5 5.9 %copy-start.76 = (pred[1016]{0:T(1024)(128)(4,1)}, pred[1016]{0:T(1024)(128)(4,1)S(1)}, u32[]{:S(2)}) copy-start(pred[1016]{0:T(1024)(128)(4,1)S(1)} %compare_and_fusion) | copy-start | bytes 3052
  48.0 3.7 %copy-start.64 = (bf16[8,127]{1,0:T(8,128)(2,1)S(1)}, bf16[8,127]{1,0:T(8,128)(2,1)}, u32[]{:S(2)}) copy-start(bf16[8,127]{1,0:T(8,128)(2,1)} %bitcast_convert_fusion) | copy-start | bytes 6100
  51.6 8.8 %copy-start.48 = (bf16[12,1,12,128]{3,2,1,0:T(8,128)(2,1)S(1)}, bf16[12,1,12,128]{3,2,1,0:T(8,128)(2,1)}, u32[]{:S(2)}) copy-start(bf16[12,1,12,128]{3,2,1,0:T(8,128)(2,1)} %get-tuple-element.783) | copy-start | bytes 110596
  51.6 14.0 %copy-start.47 = (bf16[3,128,128]{1,2,0:T(8,128)(2,1)S(1)}, bf16[3,128,128]{1,2,0:T(8,128)(2,1)}, u32[]{:S(2)}) copy-start(bf16[3,128,128]{1,2,0:T(8,128)(2,1)} %get-tuple-element.669) | copy-start | bytes 294916
  51.8 14.6 %copy-start.46 = (bf16[3,128,128]{1,2,0:T(8,128)(2,1)S(1)}, bf16[3,128,128]{1,2,0:T(8,128)(2,1)}, u32[]{:S(2)}) copy-start(bf16[3,128,128]{1,2,0:T(8,128)(2,1)} %get-tuple-element.670) | copy-start | bytes 294916
  52.7 19.5 %all-to-all-start.3 = ((bf16[8,127,128]{2,1,0:T(8,128)(2,1)}), bf16[8,127,128]{2,1,0:T(8,128)(2,1)S(1)}, u32[]{:S(2)}, u32[]{:S(2)}) async-start(bf16[8,127,128]{2,1,0:T(8,128)(2,1)} %broadcast_multiply_fusion.2), calls=%async_computation.3 | async-start | bytes 524288 | tf_op jit(solution)/shard_map/all_to_all | solution.py:128
  58.8 12.8 %copy-start.63 = (bf16[12,1,1,128]{3,2,1,0:T(2,128)(2,1)S(1)}, bf16[12,1,1,128]{3,2,1,0:T(2,128)(2,1)}, u32[]{:S(2)}) copy-start(bf16[12,1,1,128]{3,2,1,0:T(2,128)(2,1)} %get-tuple-element.781) | copy-start | bytes 9220
  119.7 2.1 copy-start.49
  119.7 2.1 copy-start.50
  119.7 2.1 copy-start.51
  119.7 2.1 copy-start.52
  119.7 2.1 copy-start.66
  119.7 2.1 copy-start.67
  119.8 2.1 copy-start.68
  119.8 2.1 copy-start.69
  119.8 2.1 copy-start.70
  119.8 2.1 copy-start.71
  119.8 2.1 copy-start.72
  119.8 2.1 copy-start.73
  119.8 2.1 copy-start.74
  119.8 2.1 copy-start.75
  121.8 24.8 %copy-start.59 = (s32[1024]{0:T(1024)S(1)}, s32[1024]{0:T(1024)}, u32[]{:S(2)}) copy-start(s32[1024]{0:T(1024)} %copy-done.58) | copy-start | bytes 12292
  122.9 27.0 %copy-start.77 = (pred[1016]{0:T(1024)(128)(4,1)S(1)}, pred[1016]{0:T(1024)(128)(4,1)}, u32[]{:S(2)}) copy-start(pred[1016]{0:T(1024)(128)(4,1)} %copy-done.76) | copy-start | bytes 3052
  146.6 3.7 %copy-start.65 = (bf16[8,127]{1,0:T(8,128)(2,1)S(1)}, bf16[8,127]{1,0:T(8,128)(2,1)}, u32[]{:S(2)}) copy-start(bf16[8,127]{1,0:T(8,128)(2,1)} %bitcast_convert_fusion) | copy-start | bytes 6100
  146.6 8.1 %copy-start.25 = (bf16[12,12,12,128]{3,2,1,0:T(8,128)(2,1)S(1)}, bf16[12,12,12,128]{3,2,1,0:T(8,128)(2,1)}, u32[]{:S(2)}) copy-start(bf16[12,12,12,128]{3,2,1,0:T(8,128)(2,1)} %copy-done.24) | copy-start | bytes 1327108
  151.2 13.1 %all-to-all-start.1 = ((bf16[8,127,128]{2,1,0:T(8,128)(2,1)}), bf16[8,127,128]{2,1,0:T(8,128)(2,1)S(1)}, u32[]{:S(2)}, u32[]{:S(2)}) async-start(bf16[8,127,128]{2,1,0:T(8,128)(2,1)} %broadcast_multiply_fusion.3), calls=%async_computation.1 | async-start | bytes 524288 | tf_op jit(solution)/shard_map/all_to_all | solution.py:128
  154.6 127.1 %all-reduce.5.cloned.1.call-start = ((), (), s32[]{:S(2)}) async-start(), calls=%async_computation.4 | async-start | bytes 3538944 | tf_op jit(solution)/shard_map/psum | solution.py:214
  181.1 2.7 copy-start.45
  181.1 4.2 %copy-start.26 = (bf16[12,12,12,128]{3,2,1,0:T(8,128)(2,1)S(1)}, bf16[12,12,12,128]{3,2,1,0:T(8,128)(2,1)}, u32[]{:S(2)}) copy-start(bf16[12,12,12,128]{3,2,1,0:T(8,128)(2,1)} %get-tuple-element.713) | copy-start | bytes 1327108
  181.1 4.2 %copy-start.27 = (bf16[12,12,12,128]{3,2,1,0:T(8,128)(2,1)S(1)}, bf16[12,12,12,128]{3,2,1,0:T(8,128)(2,1)}, u32[]{:S(2)}) copy-start(bf16[12,12,12,128]{3,2,1,0:T(8,128)(2,1)} %get-tuple-element.714) | copy-start | bytes 1327108
  181.1 4.2 %copy-start.28 = (bf16[12,12,12,128]{3,2,1,0:T(8,128)(2,1)S(1)}, bf16[12,12,12,128]{3,2,1,0:T(8,128)(2,1)}, u32[]{:S(2)}) copy-start(bf16[12,12,12,128]{3,2,1,0:T(8,128)(2,1)} %get-tuple-element.715) | copy-start | bytes 1327108
  204.3 3.2 copy-start.7
  204.4 5.9 %copy-start.17 = (bf16[1728,384]{1,0:T(8,128)(2,1)S(1)}, bf16[1728,384]{1,0:T(8,128)(2,1)}, u32[]{:S(2)}) copy-start(bf16[1728,384]{1,0:T(8,128)(2,1)} %reshape.2672) | copy-start | bytes 3981316
  204.4 5.9 %copy-start.23 = (bf16[1,1,1728,128]{3,2,1,0:T(8,128)(2,1)S(1)}, bf16[1,1,1728,128]{3,2,1,0:T(8,128)(2,1)}, u32[]{:S(2)}) copy-start(bf16[1,1,1728,128]{3,2,1,0:T(8,128)(2,1)} %param.117) | copy-start | bytes 1327108
  207.5 4.3 %copy-start.13 = (bf16[1728,384]{1,0:T(8,128)(2,1)S(1)}, bf16[1728,384]{1,0:T(8,128)(2,1)}, u32[]{:S(2)}) copy-start(bf16[1728,384]{1,0:T(8,128)(2,1)} %reshape.2674) | copy-start | bytes 3981316
  210.2 3.2 copy-start.9
  211.8 3.2 copy-start.5
  213.4 3.2 copy-start.3
  219.7 109.0 %all-reduce.7.cloned.1.call-start = ((), (), s32[]{:S(2)}) async-start(), calls=%async_computation.5 | async-start | bytes 442368 | tf_op jit(solution)/shard_map/psum | solution.py:218
  227.3 59.3 %copy-start.37 = (bf16[3,128,128]{2,1,0:T(8,128)(2,1)S(1)}, bf16[3,128,128]{2,1,0:T(8,128)(2,1)}, u32[]{:S(2)}) copy-start(bf16[3,128,128]{2,1,0:T(8,128)(2,1)} %get-tuple-element.684) | copy-start | bytes 294916
  (45 other events, 68.6 us)
Sparse Core Ops, SparseCore 0:
  219.9 61.7 all-reduce.4
  286.7 42.0 all-reduce.6
where the time goes:
time: 343 us; the launch traced here: 337 us
  waiting for transfers between devices  105 us (31%)
  local copies, waits for them, and re-layouts  102 us (30%)
  other arithmetic  43.3 us (13%)
  matrix products  31.5 us (9%)
  blocking collectives  23.5 us (7%)
  between operations  17.2 us (5%)
  starting transfers between devices  14.9 us (4%)
    psum x1, waiting for transfers between devices, body(): summed = lax.psum(flat_grad, 'region')  54.4 us
    psum x1, waiting for transfers between devices, body(): update = lax.psum(share * factor, 'scene') / lax.axis_size('scene')  40.9 us
    all_to_all x1, blocking collectives, relay(): lax.all_to_all(dealt_shell(cube, region_count, plan[2]), 'region', split_...  23.5 us
    dot_general x9, matrix products, convolve(): lax.dot_general(window, grad_block, (((0,), (0,)), ((), ())), preferred_e...  18 us
    gather x26, local copies, waits for them, and re-layouts, holder_table(): holder = jnp.take(owner_row, target, axis=0)  16.8 us
    concatenate x9, other arithmetic, convolve(): jnp.concatenate([mirror_column[:, :, 1 - shift_z:1 - shift_z + edge] for...  14.4 us
    concatenate x9, other arithmetic, column_window(): jnp.concatenate([column[:, :, 1 + shift_z:1 + shift_z + edge] for shift_z...  13 us
    scatter x52, local copies, waits for them, and re-layouts, assemble(): padded = padded.at[spans[0][0]:spans[0][1], spans[1][0]:spans[1][1], span...  10.4 us
  transfers between devices with their start and end apart: 5, of which 3 were waited for; matrix products, arithmetic and copies ran while one was open for 14% of the time, Pallas kernels for 0%

commit v1 on v0

--- a/solution.py
+++ b/solution.py
@@ -1,9 +1,12 @@
+import functools
 import math
 
 import jax
 import jax.numpy as jnp
 import numpy as np
 from jax import lax
+from jax.experimental import pallas as pl
+from jax.experimental.pallas import tpu as pltpu
 from jax.sharding import PartitionSpec as P
 
 BS = 12
@@ -219,6 +222,384 @@
     return (block_output.reshape(features.shape), input_grad.reshape(cotangent.shape), update)
 
 
+PLANE = BS * BS
+ZPAD = 16
+ROWS = BS * ZPAD
+WIDE = (BS + 2) * ZPAD
+EDGE_ROWS = 4 * BS
+STACK = 256
+FACE_A, FACE_D, FACE_C, FACE_B = 0, BS, 2 * BS, 3 * BS
+
+
+def extract_table():
+    table = np.zeros((EDGE_ROWS, PLANE), np.float32)
+    for i in range(BS):
+        table[FACE_A + i, i] = 1
+        table[FACE_D + i, i * BS + BS - 1] = 1
+        table[FACE_C + i, i * BS] = 1
+        table[FACE_B + i, (BS - 1) * BS + i] = 1
+    return table
+
+
+def spread_table():
+    ym, yp, zn = PLANE, PLANE + 16, PLANE + 32
+    ymz, ypz = zn + EDGE_ROWS, zn + EDGE_ROWS + 16
+    table = np.zeros((GZ, 3, BS + 2, ZPAD, STACK), np.float32)
+    for bz in range(GZ):
+        for c in range(3):
+            for y in range(-1, BS + 1):
+                for row in range(BS + 2):
+                    z = row - 1 + c - 1
+                    if z < -1 or z > BS:
+                        continue
+                    y_in, z_in = 0 <= y < BS, 0 <= z < BS
+                    if not z_in and (z < 0) != (bz == 1):
+                        continue
+                    near = 0 if z > 0 else BS - 1
+                    if y_in and z_in:
+                        col = y * BS + z
+                    elif z_in:
+                        col = ym + FACE_B - 32 + z if y < 0 else yp + FACE_A + z
+                    elif y_in:
+                        col = zn + (FACE_C if z > 0 else FACE_D) + y
+                    else:
+                        col = ymz + FACE_B - 32 + near if y < 0 else ypz + FACE_A + near
+                    table[bz, c, y + 1, row, col] = 1
+    return table
+
+
+def fused_kernel(
+    feat, mask, cot, gain, weight, near, extract, spread, own_spread, squeeze,
+    out, grad_in, update,
+    g_msg, a_msg, g_stack, a_stack, g_wide, a_wide, own_wide, own_turned,
+    normed_s, slope_s, rinv_s, part, from_twin, pair16, pair_own, from_z, squares, shares, factors,
+    halo_send, halo_recv, twin_send, twin_recv, z_send, z_recv, sq_send, sq_recv, sh_send, sh_recv, fa_send, fa_recv,
+):
+    f32, bf16 = jnp.float32, jnp.bfloat16
+    me = lax.axis_index("region")
+    scene = lax.axis_index("scene")
+    core = lax.rem(me, 2)
+    chip = lax.div(me, 2)
+    chips = GY * GZ // 2
+    twin = 2 * chip + 1 - core
+    share_rows = TAPS * 128 // (GY * GZ)
+
+    def remote(src, dst, send, recv, **where):
+        return pltpu.make_async_remote_copy(
+            src_ref=src, dst_ref=dst, send_sem=send, recv_sem=recv,
+            device_id=where, device_id_type=pl.DeviceIdType.MESH,
+        )
+
+    barrier = pltpu.get_barrier_semaphore()
+    for k in range(1, 8):
+        pl.semaphore_signal(barrier, inc=1, device_id={"region": lax.rem(me + k, 8)}, device_id_type=pl.DeviceIdType.MESH)
+    for k in range(1, 4):
+        pl.semaphore_signal(barrier, inc=1, device_id={"scene": lax.rem(scene + k, 4)}, device_id_type=pl.DeviceIdType.MESH)
+
+    def at_plane(x, step):
+        return pl.ds(pl.multiple_of(x * step, step), step)
+
+    def grad_plane(x, carry):
+        rows = at_plane(x, PLANE)
+        g = cot[rows, :] * mask[rows, :]
+        g_stack[x, 0:PLANE, :] = g
+        g_msg[me, at_plane(x, EDGE_ROWS), :] = jnp.dot(extract[...], g, preferred_element_type=f32).astype(bf16)
+        return carry
+
+    lax.fori_loop(0, BS, grad_plane, 0, unroll=2)
+    pl.semaphore_wait(barrier, 10)
+
+    def halo_copy(which, msg, index, slot, target):
+        return remote(msg.at[slot], msg.at[slot], halo_send.at[which, index], halo_recv.at[which, slot], region=target)
+
+    def start_halo(which, msg):
+        for k in (2, 1, 3):
+            halo_copy(which, msg, k - 1, me, 2 * lax.rem(chip + k, chips) + core).start()
+        halo_copy(which, msg, 3, me, twin).start()
+
+    def pass_halo(which, msg):
+        for k in (1, 3, 2):
+            slot = 2 * lax.rem(chip + chips - k, chips) + core
+            halo_copy(which, msg, 0, slot, twin).wait_recv()
+            halo_copy(which, msg, 3 + k, slot, twin).start()
+
+    def end_halo(which, msg):
+        for k in range(4):
+            slot = 2 * lax.rem(chip + k, chips) + 1 - core
+            halo_copy(which, msg, 0, slot, twin).wait_recv()
+
+    start_halo(0, g_msg)
+    g_msg[8] = jnp.zeros(g_msg.shape[1:], bf16)
+    a_msg[8] = jnp.zeros(a_msg.shape[1:], bf16)
+
+    def act_plane(x, carry):
+        rows = at_plane(x, PLANE)
+        inputs = feat[rows, :].astype(f32)
+        rinv = lax.rsqrt(jnp.mean(inputs * inputs, axis=-1, keepdims=True) + NORM_EPSILON)
+        normed = inputs * rinv
+        pre = normed * gain[...]
+        slope = 1.0 / (1.0 + jnp.exp(-pre))
+        kept = mask[rows, :].astype(f32)
+        act = (pre * slope * kept).astype(bf16)
+        normed_s[rows, :] = normed
+        slope_s[rows, :] = kept * (slope * (1.0 + pre * (1.0 - slope))) * gain[...]
+        rinv_s[rows, :] = jnp.broadcast_to(rinv, normed.shape)
+        a_stack[x, 0:PLANE, :] = act
+        a_msg[me, at_plane(x, EDGE_ROWS), :] = jnp.dot(extract[...], act, preferred_element_type=f32).astype(bf16)
+        return carry
+
+    lax.fori_loop(0, BS, act_plane, 0, unroll=2)
+    start_halo(1, a_msg)
+
+    def own_plane(x, carry):
+        moved = jnp.dot(own_spread[...], a_stack[x, 0:PLANE, :], preferred_element_type=f32).astype(bf16)
+        for c in range(3):
+            own_wide[at_plane(x, ROWS), c * 128 : (c + 1) * 128] = moved[c * ROWS : (c + 1) * ROWS]
+        return carry
+
+    lax.fori_loop(0, BS, own_plane, 0, unroll=2)
+    turn = 4 * ROWS
+    for i in range(3):
+        for c in range(3):
+            own_turned[c * 128 : (c + 1) * 128, i * turn : (i + 1) * turn] = own_wide[
+                i * turn : (i + 1) * turn, c * 128 : (c + 1) * 128
+            ].T
+
+    def widen(msg, stack, wide):
+        wide[0] = jnp.zeros(wide.shape[1:], bf16)
+        wide[BS + 1] = jnp.zeros(wide.shape[1:], bf16)
+
+        def plane(x, carry):
+            low = pl.ds(pl.multiple_of(x * EDGE_ROWS, 16), 16)
+            high = pl.ds(pl.multiple_of(x * EDGE_ROWS + 32, 16), 16)
+            stack[x, PLANE : PLANE + 16, :] = msg[near[0], high, :]
+            stack[x, PLANE + 16 : PLANE + 32, :] = msg[near[1], low, :]
+            stack[x, PLANE + 32 : PLANE + 80, :] = msg[near[2], at_plane(x, EDGE_ROWS), :]
+            stack[x, PLANE + 80 : PLANE + 96, :] = msg[near[3], high, :]
+            stack[x, PLANE + 96 : PLANE + 112, :] = msg[near[4], low, :]
+            moved = jnp.dot(spread[near[5]], stack[x], preferred_element_type=f32).astype(bf16)
+            for c in range(3):
+                wide[x + 1, :, c * 128 : (c + 1) * 128] = moved[c * WIDE : (c + 1) * WIDE]
+            return carry
+
+        lax.fori_loop(0, BS, plane, 0, unroll=2)
+
+    pass_halo(0, g_msg)
+    end_halo(0, g_msg)
+    widen(g_msg, g_stack, g_wide)
+
+    def window(a, b):
+        return g_wide[1 - a : 1 - a + BS, (1 - b) * ZPAD : (1 - b) * ZPAD + ROWS, 128:256].reshape(BS * ROWS, 128)
+
+    for first in range(0, 9, 2):
+        group = list(range(first, min(first + 2, 9)))
+        side = [window(*COLUMNS[i]) for i in group]
+        rhs = jnp.concatenate(side, axis=1) if len(side) > 1 else side[0]
+        term = jnp.dot(own_turned[...], rhs, preferred_element_type=f32)
+        for j, i in enumerate(group):
+            part[3 * i * 128 : (3 * i + 3) * 128, :] = term[:, j * 128 : (j + 1) * 128]
+
+    def share_of(index):
+        return pl.ds(pl.multiple_of(index * share_rows, 16), share_rows)
+
+    def twin_copy(q):
+        return remote(part.at[share_of(2 * q + 1 - core)], from_twin.at[q], twin_send.at[q], twin_recv.at[q], region=twin)
+
+    for q in range(chips):
+        twin_copy(q).start()
+    pass_halo(1, a_msg)
+
+    def z_copy(k):
+        target = lax.rem(chip + k, chips)
+        return remote(pair16.at[target], from_z.at[k - 1], z_send.at[k - 1], z_recv.at[k - 1], region=2 * target + core)
+
+    for q in range(chips):
+        twin_copy(q).wait_recv()
+    for k in (2, 1, 3):
+        q = lax.rem(chip + k, chips)
+        pair16[q] = (part[share_of(2 * q + core), :] + from_twin[q]).astype(bf16)
+        z_copy(k).start()
+    pair_own[...] = part[share_of(me), :] + from_twin[chip]
+
+    count = 3
+
+    def convolve_planes(wide, taps, x0, transposed):
+        total = None
+        for a in range(3):
+            lhs = jnp.concatenate(
+                [wide[pl.ds(x0 + a, count), b * ZPAD : b * ZPAD + ROWS, :].reshape(count * ROWS, 384) for b in range(3)],
+                axis=1,
+            )
+            if transposed:
+                rhs = jnp.concatenate([taps[26 - 9 * a - j] for j in range(9)], axis=1)
+                term = lax.dot_general(lhs, rhs, (((1,), (1,)), ((), ())), preferred_element_type=f32)
+            else:
+                term = jnp.dot(lhs, taps[9 * a : 9 * a + 9].reshape(9 * 128, 128), preferred_element_type=f32)
+            total = term if total is None else total + term
+        planes = []
+        for i in range(count):
+            piece = total[i * ROWS : (i + 1) * ROWS]
+            high = piece.astype(bf16)
+            rest = (piece - high.astype(f32)).astype(bf16)
+            planes.append(jnp.dot(squeeze[...], jnp.concatenate([high, rest], axis=0), preferred_element_type=f32))
+        return planes
+
+    def backward_planes(step, carry):
+        x0 = step * count
+        for i, back in enumerate(convolve_planes(g_wide, weight, x0, True)):
+            rows = at_plane(x0 + i, PLANE)
+            normed = normed_s[rows, :]
+            dnorm = back * slope_s[rows, :]
+            level = jnp.mean(dnorm * normed, axis=-1, keepdims=True)
+            grad_in[rows, :] = (cot[rows, :].astype(f32) + rinv_s[rows, :] * (dnorm - normed * level)).astype(bf16)
+        return carry
+
+    lax.fori_loop(0, BS // count, backward_planes, 0)
+
+    end_halo(1, a_msg)
+    widen(a_msg, a_stack, a_wide)
+
+    def z_wait(k):
+        z_copy(k).wait_recv()
+
+    for k in (1, 3, 2):
+        z_wait(k)
+    share = pair_own[...] + from_z[0].astype(f32) + from_z[1].astype(f32) + from_z[2].astype(f32)
+    squares[me] = jnp.sum((share * share).reshape(share_rows // 8, 8, 128), axis=0)
+    shares[scene] = share.astype(bf16)
+
+    def sq_copy(k):
+        return remote(squares.at[me], squares.at[me], sq_send.at[k - 1], sq_recv.at[k - 1], region=lax.rem(me + k, 8))
+
+    def sq_arrival(k):
+        slot = lax.rem(me + 8 - k, 8)
+        return remote(squares.at[slot], squares.at[slot], sq_send.at[k - 1], sq_recv.at[k - 1], region=slot)
+
+    def scene_copy(buf, send, recv, k):
+        return remote(buf.at[scene], buf.at[scene], send.at[k - 1], recv.at[k - 1], scene=lax.rem(scene + k, 4))
+
+    def scene_arrival(buf, send, recv, k):
+        slot = lax.rem(scene + 4 - k, 4)
+        return remote(buf.at[slot], buf.at[slot], send.at[k - 1], recv.at[k - 1], scene=slot)
+
+    for k in range(1, 8):
+        sq_copy(k).start()
+    for k in range(1, 4):
+        scene_copy(shares, sh_send, sh_recv, k).start()
+
+    def forward_planes(step, carry):
+        x0 = step * count
+        for i, ahead in enumerate(convolve_planes(a_wide, weight, x0, False)):
+            rows = at_plane(x0 + i, PLANE)
+            out[rows, :] = (feat[rows, :].astype(f32) + ahead * mask[rows, :].astype(f32)).astype(bf16)
+        return carry
+
+    lax.fori_loop(0, 1, forward_planes, 0)
+    for k in range(1, 8):
+        sq_arrival(k).wait_recv()
+    total = jnp.sum(jnp.sum(squares[...], axis=0), keepdims=True)
+    limit = math.sqrt(TAPS * 128 * 128)
+    factors[scene] = jnp.broadcast_to(jnp.minimum(1.0, limit * lax.rsqrt(total)), (8, 128))
+    for k in range(1, 4):
+        scene_copy(factors, fa_send, fa_recv, k).start()
+    lax.fori_loop(1, BS // count, forward_planes, 0)
+    for k in range(1, 4):
+        scene_arrival(shares, sh_send, sh_recv, k).wait_recv()
+        scene_arrival(factors, fa_send, fa_recv, k).wait_recv()
+    result = jnp.zeros((share_rows, 128), f32)
+    for s in range(4):
+        result = result + factors[s, 0:1, :] * shares[s].astype(f32)
+    update[...] = result * 0.25
+
+    for which, msg in ((0, g_msg), (1, a_msg)):
+        for index in range(7):
+            halo_copy(which, msg, index, me, twin).wait_send()
+    for q in range(chips):
+        twin_copy(q).wait_send()
+    for k in range(1, 4):
+        z_copy(k).wait_send()
+        scene_copy(shares, sh_send, sh_recv, k).wait_send()
+        scene_copy(factors, fa_send, fa_recv, k).wait_send()
+    for k in range(1, 8):
+        sq_copy(k).wait_send()
+
+
+def fused_body(features, voxel_mask, cotangent, norm_gain, conv_weight, block_owner):
+    f32, bf16 = jnp.float32, jnp.bfloat16
+    width = features.shape[-1]
+    slots = lax.axis_size("region")
+    spread = spread_table()
+    own = spread[0, :, 1 : 1 + BS, :, :PLANE].reshape(3 * ROWS, PLANE)
+    squeeze = np.zeros((BS, BS, BS, ZPAD), np.float32)
+    for y in range(BS):
+        for z in range(BS):
+            squeeze[y, z, y, z + 1] = 1
+    squeeze = squeeze.reshape(PLANE, ROWS)
+    squeeze = np.concatenate([squeeze, squeeze], axis=1)
+    spread = spread.reshape(GZ, 3 * WIDE, STACK)
+    owner = block_owner[0]
+    block = jnp.sum(jnp.where(owner == lax.axis_index("region"), jnp.arange(slots, dtype=jnp.int32), 0))
+    by, bz = block // GZ, block % GZ
+
+    def holder(y, z):
+        inside = (y >= 0) & (y < GY)
+        return jnp.where(inside, owner[jnp.clip(y * GZ + z, 0, slots - 1)], slots)
+
+    near = jnp.stack(
+        [holder(by - 1, bz), holder(by + 1, bz), holder(by, 1 - bz), holder(by - 1, 1 - bz), holder(by + 1, 1 - bz), bz]
+    ).astype(jnp.int32)
+    voxels = BS * BS * BS
+    mask = jnp.broadcast_to(voxel_mask[0, 0].astype(bf16)[:, None], (voxels, width))
+    vmem = pl.BlockSpec(memory_space=pltpu.VMEM)
+    share_rows = TAPS * width // slots
+    sem = pltpu.SemaphoreType.DMA
+    out, grad_in, update = pl.pallas_call(
+        fused_kernel,
+        out_shape=(
+            jax.ShapeDtypeStruct((voxels, width), bf16),
+            jax.ShapeDtypeStruct((voxels, width), bf16),
+            jax.ShapeDtypeStruct((share_rows, width), f32),
+        ),
+        in_specs=[vmem] * 5 + [pl.BlockSpec(memory_space=pltpu.SMEM)] + [vmem] * 4,
+        out_specs=(vmem, vmem, vmem),
+        scratch_shapes=[
+            pltpu.VMEM((slots + 1, BS * EDGE_ROWS, width), bf16),
+            pltpu.VMEM((slots + 1, BS * EDGE_ROWS, width), bf16),
+            pltpu.VMEM((BS, STACK, width), bf16),
+            pltpu.VMEM((BS, STACK, width), bf16),
+            pltpu.VMEM((BS + 2, WIDE, 3 * width), bf16),
+            pltpu.VMEM((BS + 2, WIDE, 3 * width), bf16),
+            pltpu.VMEM((BS * ROWS, 3 * width), bf16),
+            pltpu.VMEM((3 * width, BS * ROWS), bf16),
+            pltpu.VMEM((voxels, width), f32),
+            pltpu.VMEM((voxels, width), f32),
+            pltpu.VMEM((voxels, width), f32),
+            pltpu.VMEM((TAPS * width, width), f32),
+            pltpu.VMEM((slots // 2, share_rows, width), f32),
+            pltpu.VMEM((slots // 2, share_rows, width), bf16),
+            pltpu.VMEM((share_rows, width), f32),
+            pltpu.VMEM((slots // 2 - 1, share_rows, width), bf16),
+            pltpu.VMEM((slots, 8, width), f32),
+            pltpu.VMEM((4, share_rows, width), bf16),
+            pltpu.VMEM((4, 8, width), f32),
+            sem((2, 7)), sem((2, slots)),
+            sem((slots // 2,)), sem((slots // 2,)),
+            sem((3,)), sem((3,)),
+            sem((7,)), sem((7,)),
+            sem((3,)), sem((3,)),
+            sem((3,)), sem((3,)),
+        ],
+        compiler_params=pltpu.CompilerParams(
+            collective_id=0, has_side_effects=True, vmem_limit_bytes=50 * 1024 * 1024
+        ),
+        cost_estimate=pl.CostEstimate(flops=5_000_000_000, bytes_accessed=4_000_000, transcendentals=300_000),
+    )(
+        features[0, 0], mask, cotangent[0, 0], norm_gain[None, :], conv_weight, near,
+        jnp.asarray(extract_table(), bf16), jnp.asarray(spread, bf16), jnp.asarray(own, bf16), jnp.asarray(squeeze, bf16),
+    )
+    return (out.reshape(features.shape), grad_in.reshape(cotangent.shape), update)
+
+
 def solution(mesh):
     in_specs = (
         P("scene", "region", None, None),
@@ -233,4 +614,5 @@
         P("scene", "region", None, None),
         P("region", None),
     )
-    return jax.shard_map(body, mesh=mesh, in_specs=in_specs, out_specs=out_specs, check_vma=False)
+    chosen = fused_body if mesh.shape["region"] == GY * GZ else body
+    return jax.shard_map(chosen, mesh=mesh, in_specs=in_specs, out_specs=out_specs, check_vma=False)

time: 343 us -> 71.9 us (0.21); the launches traced: 337 us -> 71.5 us
  waiting for transfers between devices: 105 us -> 0 us
  local copies, waits for them, and re-layouts: 102 us -> 7.77 us
  Pallas kernels: 0 us -> 55.1 us
  other arithmetic: 43.3 us -> 2.07 us
  matrix products: 31.5 us -> 0 us
  blocking collectives: 23.5 us -> 0 us
  starting transfers between devices: 14.9 us -> 0 us
  between operations: 17.2 us -> 6.51 us
    psum x2 -> x0, waiting for transfers between devices: 95.3 us -> none  [the longest x1 54.4 us: body(): summed = lax.psum(flat_grad, 'region')]
    pallas_call x0 -> x1, Pallas kernels: none -> 55.1 us  [fused_body(): pl.pallas_call(fused_kernel, out_shape=(jax.ShapeDtypeStruct((voxels, wid...]
    dot_general x27 -> x0, matrix products: 31.5 us -> none  [the longest x9 18 us: convolve(): lax.dot_general(window, grad_block, (((0,), (0,)), ((), ())), preferred_e...]
    reshape x36 -> x0, local copies, waits for them, and re-layouts: 27.5 us -> none  [the longest x9 10.4 us: convolve(): mirror = jnp.concatenate([mirror_column[:, :, 1 - shift_z:1 - shift_z + e...]
    concatenate x18 -> x0, other arithmetic: 27.5 us -> none  [the longest x9 14.4 us: convolve(): jnp.concatenate([mirror_column[:, :, 1 - shift_z:1 - shift_z + edge] for...]
    gather x30 -> x0, local copies, waits for them, and re-layouts: 24.1 us -> none  [the longest x26 16.8 us: holder_table(): holder = jnp.take(owner_row, target, axis=0)]
    all_to_all x1 -> x0, blocking collectives: 23.5 us -> none  [relay(): lax.all_to_all(dealt_shell(cube, region_count, plan[2]), 'region', split_...]
    slice x28 -> x0, local copies, waits for them, and re-layouts: 17 us -> none  [the longest x2 7.11 us: convolve(): mirror_column[:, :, 1 - shift_z:1 - shift_z + edge]]
  transfers between devices with their start and end apart: 5 -> 0, of which waited for: 3 -> 0; matrix products, arithmetic and copies ran while one was open for 14% -> 0% of each run, Pallas kernels for 0% -> 0%
where the time goes in v1:
time: 71.9 us; the launch traced here: 71.5 us
  Pallas kernels  55.1 us (77%)
  local copies, waits for them, and re-layouts  7.77 us (11%)
  between operations  6.51 us (9%)
  other arithmetic  2.07 us (3%)
    pallas_call x1, Pallas kernels, fused_body(): pl.pallas_call(fused_kernel, out_shape=(jax.ShapeDtypeStruct((voxels, wid...  55.1 us
    unnamed x17, local copies, waits for them, and re-layouts  5.87 us
    dynamic_slice x1, local copies, waits for them, and re-layouts, holder(): return jnp.where(inside, owner[jnp.clip(y * GZ + z, 0, slots - 1)], slots)  1.53 us

profile of v1, /device:TPU:0, one launch (start us, length us, event | category | flops | bytes accessed | tf_op | source)
XLA Modules:
  0.0 71.5 jit_solution(16176987692485931051)
XLA Ops:
  0.6 0.0 copy-start
  0.6 1.3 %fusion = s32[]{:T(128)} fusion(s32[1,8]{1,0:T(1,128)} %param.15, s32[]{:T(128)S(6)} %axis_index.12), kind=kLoop, calls=%fused_computation.7 | loop fusion | flops 23 | bytes 40 | tf_op jit(solution)/shard_map/reduce_sum | solution.py:541
  4.6 1.5 %constant_dynamic-slice_fusion = (s32[1,1]{1,0:T(1,128)}, s32[1,1]{1,0:T(1,128)}, s32[1,1]{1,0:T(1,128)}, s32[1,1]{1,0:T(1,128)}, s32[1,1]{1,0:T(1,128)}) fusion(s32[1,8]{1,0:T(1,128)} %param.15, s32[]{:T(128)S(6)} %min.20, s32[]{:T(128)S(6)} %min.18, s32[]{:T(128)S(6)} %min.17, s32[]{:T(128)S(6)} %min.16, s32[]{:T(128)S(6)} %min.19), kind=kLoop, calls=%fused_computation.2 | loop fusion | bytes 60 | tf_op jit(solution)/shard_map/dynamic_slice | solution.py:546
  9.3 0.1 stack.27.near
  9.4 0.7 %convert_reduce_fusion = bf16[1728]{0:T(1024)(128)(2,1)S(1)} fusion(s32[1,1,1728]{2,1,0:T(1,128)} %param.11), kind=kLoop, calls=%fused_computation | loop fusion | flops 1728 | bytes 10368 | tf_op jit(solution)/shard_map/convert_element_type | solution.py:552
  10.1 0.0 copy-start.2
  10.2 0.0 copy-start.5
  10.2 0.0 copy-start.6
  10.2 0.3 broadcast_in_dim.13.mask
  10.5 0.0 copy-done
  10.5 0.3 copy-done.2
  10.8 0.3 copy-done.5
  11.1 0.0 copy-done.6
  11.1 0.0 copy-start.1
  11.1 1.0 %copy-done.1 = bf16[1,1,1728,128]{3,2,1,0:T(8,128)(2,1)S(1)} copy-done((bf16[1,1,1728,128]{3,2,1,0:T(8,128)(2,1)S(1)}, bf16[1,1,1728,128]{3,2,1,0:T(8,128)(2,1)}, u32[]{:S(2)}) %copy-start.1) | copy-done | bytes 442392
  12.1 0.0 copy-start.3
  12.1 1.1 %copy-done.3 = bf16[2,672,256]{2,1,0:T(8,128)(2,1)S(1)} copy-done((bf16[2,672,256]{2,1,0:T(8,128)(2,1)S(1)}, bf16[2,672,256]{2,1,0:T(8,128)(2,1)}, u32[]{:S(2)}) %copy-start.3) | copy-done | bytes 688152
  13.2 0.0 copy-start.4
  13.2 1.0 %copy-done.4 = bf16[576,144]{1,0:T(8,128)(2,1)S(1)} copy-done((bf16[576,144]{1,0:T(8,128)(2,1)S(1)}, bf16[576,144]{1,0:T(8,128)(2,1)}, u32[]{:S(2)}) %copy-start.4) | copy-done | bytes 165912
  14.1 55.1 %shard_map.121 = (bf16[1728,128]{1,0:T(8,128)(2,1)S(1)}, bf16[1728,128]{1,0:T(8,128)(2,1)S(1)}, f32[432,128]{1,0:T(8,128)S(1)}) custom-call(bf16[1728,128]{1,0:T(8,128)(2,1)S(1)} %bitcast.22, bf16[1728,128]{1,0:T(8,128)(2,1)S(1)} %broadcast_in_dim.13.mask, bf16[1728,128]{1,0:T(8,128)(2,1)S(1)} %bitcast.23, f32[1,128]{1,0:T(1,128)S(1)} %bitcast.24, ...), custom_call_target="tpu_custom_call" | custom-call | flops 5000000000 | bytes 4000000 | tf_op jit(solution)/shard_map/pallas_call | solution.py:556
  69.2 0.8 %copy.16 = bf16[1,1,1728,128]{3,2,1,0:T(8,128)(2,1)} copy(bf16[1,1,1728,128]{3,2,1,0:T(8,128)(2,1)S(1)} %bitcast.21) | data formatting | bytes 884736
  70.0 0.8 %copy.17 = bf16[1,1,1728,128]{3,2,1,0:T(8,128)(2,1)} copy(bf16[1,1,1728,128]{3,2,1,0:T(8,128)(2,1)S(1)} %bitcast.20) | data formatting | bytes 884736
  70.8 0.7 copy.18
Async XLA Ops:
  0.6 9.8 %copy-start = (bf16[1,1,1728,128]{3,2,1,0:T(8,128)(2,1)S(1)}, bf16[1,1,1728,128]{3,2,1,0:T(8,128)(2,1)}, u32[]{:S(2)}) copy-start(bf16[1,1,1728,128]{3,2,1,0:T(8,128)(2,1)} %param.10) | copy-start | bytes 1327108
  10.1 0.7 copy-start.2
  10.2 0.9 %copy-start.5 = (bf16[144,384]{1,0:T(8,128)(2,1)S(1)}, bf16[144,384]{1,0:T(8,128)(2,1)}, u32[]{:S(2)}) copy-start(bf16[144,384]{1,0:T(8,128)(2,1)} %constant.58.clone.squeeze) | copy-start | bytes 331780
  10.2 0.9 %copy-start.6 = (bf16[48,144]{1,0:T(8,128)(2,1)S(1)}, bf16[48,144]{1,0:T(8,128)(2,1)}, u32[]{:S(2)}) copy-start(bf16[48,144]{1,0:T(8,128)(2,1)} %constant.55.clone.extract) | copy-start | bytes 41476
  11.1 1.0 %copy-start.1 = (bf16[1,1,1728,128]{3,2,1,0:T(8,128)(2,1)S(1)}, bf16[1,1,1728,128]{3,2,1,0:T(8,128)(2,1)}, u32[]{:S(2)}) copy-start(bf16[1,1,1728,128]{3,2,1,0:T(8,128)(2,1)} %param.12) | copy-start | bytes 1327108
  12.1 1.1 %copy-start.3 = (bf16[2,672,256]{2,1,0:T(8,128)(2,1)S(1)}, bf16[2,672,256]{2,1,0:T(8,128)(2,1)}, u32[]{:S(2)}) copy-start(bf16[2,672,256]{2,1,0:T(8,128)(2,1)} %constant.56.clone.spread) | copy-start | bytes 2064388
  13.2 1.0 %copy-start.4 = (bf16[576,144]{1,0:T(8,128)(2,1)S(1)}, bf16[576,144]{1,0:T(8,128)(2,1)}, u32[]{:S(2)}) copy-start(bf16[576,144]{1,0:T(8,128)(2,1)} %constant.57.clone.own_spread) | copy-start | bytes 497668

commit v2 on v1

--- a/solution.py
+++ b/solution.py
@@ -227,7 +227,9 @@
 ROWS = BS * ZPAD
 WIDE = (BS + 2) * ZPAD
 EDGE_ROWS = 4 * BS
-STACK = 256
+STACK = PLANE + EDGE_ROWS
+PICKED = 16 * 7
+GROUP = BS // 4
 FACE_A, FACE_D, FACE_C, FACE_B = 0, BS, 2 * BS, 3 * BS
 
 
@@ -241,9 +243,22 @@
     return table
 
 
+def compact_table():
+    ym, yp, zn = 0, 16, 32
+    ymz, ypz = zn + EDGE_ROWS, zn + EDGE_ROWS + 16
+    table = np.zeros((GZ, EDGE_ROWS, PICKED), np.float32)
+    for bz in range(GZ):
+        near = 0 if bz == 0 else BS - 1
+        for i in range(BS):
+            table[bz, i, ym + FACE_B - 32 + i] = 1
+            table[bz, BS + i, yp + FACE_A + i] = 1
+            table[bz, 2 * BS + i, zn + (FACE_C if bz == 0 else FACE_D) + i] = 1
+        table[bz, 3 * BS, ymz + FACE_B - 32 + near] = 1
+        table[bz, 3 * BS + 1, ypz + FACE_A + near] = 1
+    return table
+
+
 def spread_table():
-    ym, yp, zn = PLANE, PLANE + 16, PLANE + 32
-    ymz, ypz = zn + EDGE_ROWS, zn + EDGE_ROWS + 16
     table = np.zeros((GZ, 3, BS + 2, ZPAD, STACK), np.float32)
     for bz in range(GZ):
         for c in range(3):
@@ -255,25 +270,26 @@
                     y_in, z_in = 0 <= y < BS, 0 <= z < BS
                     if not z_in and (z < 0) != (bz == 1):
                         continue
-                    near = 0 if z > 0 else BS - 1
                     if y_in and z_in:
                         col = y * BS + z
                     elif z_in:
-                        col = ym + FACE_B - 32 + z if y < 0 else yp + FACE_A + z
+                        col = PLANE + z if y < 0 else PLANE + BS + z
                     elif y_in:
-                        col = zn + (FACE_C if z > 0 else FACE_D) + y
+                        col = PLANE + 2 * BS + y
                     else:
-                        col = ymz + FACE_B - 32 + near if y < 0 else ypz + FACE_A + near
+                        col = PLANE + 3 * BS if y < 0 else PLANE + 3 * BS + 1
                     table[bz, c, y + 1, row, col] = 1
     return table
 
 
 def fused_kernel(
-    feat, mask, cot, gain, weight, near, extract, spread, own_spread, squeeze,
+    feat_h, cot_h, weight_h, extract_h, compact_h, own_spread_h, spread_h, squeeze_h, mask, gain, owner,
     out, grad_in, update,
-    g_msg, a_msg, g_stack, a_stack, g_wide, a_wide, own_wide, own_turned,
+    feat, cot, weight, extract, compact, own_spread, spread, squeeze,
+    g_msg, a_msg, deal, deliver, halo, g_stack, a_stack, g_wide, a_wide, own_wide, own_turned,
     normed_s, slope_s, rinv_s, part, from_twin, pair16, pair_own, from_z, squares, shares, factors,
-    halo_send, halo_recv, twin_send, twin_recv, z_send, z_recv, sq_send, sq_recv, sh_send, sh_recv, fa_send, fa_recv,
+    load_sem, deal_send, deal_recv, halo_send, halo_recv,
+    twin_send, twin_recv, z_send, z_recv, sq_send, sq_recv, sh_send, sh_recv, fa_send, fa_recv,
 ):
     f32, bf16 = jnp.float32, jnp.bfloat16
     me = lax.axis_index("region")
@@ -290,6 +306,17 @@
             device_id=where, device_id_type=pl.DeviceIdType.MESH,
         )
 
+    loads = [
+        pltpu.make_async_copy(src, dst, load_sem.at[i])
+        for i, (src, dst) in enumerate(
+            (
+                (cot_h, cot), (extract_h, extract), (feat_h, feat), (compact_h, compact),
+                (own_spread_h, own_spread), (spread_h, spread), (weight_h, weight), (squeeze_h, squeeze),
+            )
+        )
+    ]
+    for load in loads:
+        load.start()
     barrier = pltpu.get_barrier_semaphore()
     for k in range(1, 8):
         pl.semaphore_signal(barrier, inc=1, device_id={"region": lax.rem(me + k, 8)}, device_id_type=pl.DeviceIdType.MESH)
@@ -299,38 +326,77 @@
     def at_plane(x, step):
         return pl.ds(pl.multiple_of(x * step, step), step)
 
+    def neighbours(slot):
+        block = jnp.int32(0)
+        for k in range(1, GY * GZ):
+            block = block + jnp.where(owner[0, k] == slot, k, 0)
+        by, bz = lax.div(block, GZ), lax.rem(block, GZ)
+
+        def holder(y, z):
+            held = owner[0, jnp.clip(y * GZ + z, 0, GY * GZ - 1)]
+            return jnp.where((y >= 0) & (y < GY), held, GY * GZ)
+
+        return (
+            holder(by - 1, bz), holder(by + 1, bz), holder(by, 1 - bz),
+            holder(by - 1, 1 - bz), holder(by + 1, 1 - bz), bz,
+        )
+
     def grad_plane(x, carry):
         rows = at_plane(x, PLANE)
         g = cot[rows, :] * mask[rows, :]
         g_stack[x, 0:PLANE, :] = g
-        g_msg[me, at_plane(x, EDGE_ROWS), :] = jnp.dot(extract[...], g, preferred_element_type=f32).astype(bf16)
+        g_msg[at_plane(x, EDGE_ROWS), :] = jnp.dot(extract[...], g, preferred_element_type=f32).astype(bf16)
         return carry
 
+    loads[0].wait()
+    loads[1].wait()
     lax.fori_loop(0, BS, grad_plane, 0, unroll=2)
     pl.semaphore_wait(barrier, 10)
 
-    def halo_copy(which, msg, index, slot, target):
-        return remote(msg.at[slot], msg.at[slot], halo_send.at[which, index], halo_recv.at[which, slot], region=target)
-
-    def start_halo(which, msg):
+    deal_rows = GROUP * EDGE_ROWS
+
+    def deal_copy(which, msg, k):
+        q = lax.rem(chip + k, chips)
+        return remote(
+            msg.at[at_plane(q, deal_rows)], deal.at[me], deal_send.at[which, k], deal_recv.at[me], region=2 * q + which
+        )
+
+    def start_deal(which, msg):
         for k in (2, 1, 3):
-            halo_copy(which, msg, k - 1, me, 2 * lax.rem(chip + k, chips) + core).start()
-        halo_copy(which, msg, 3, me, twin).start()
-
-    def pass_halo(which, msg):
+            deal_copy(which, msg, k).start()
+
+        @pl.when(core != which)
+        def _():
+            deal_copy(which, msg, 0).start()
+
+        @pl.when(core == which)
+        def _():
+            deal[me] = msg[at_plane(chip, deal_rows), :]
+
+    def deal_arrival(slot):
+        return remote(deal.at[slot], deal.at[slot], deal_send.at[0, 0], deal_recv.at[slot], region=twin)
+
+    def halo_copy(k):
+        slot = lax.rem(me + k, 8)
+        return remote(
+            deliver.at[slot], halo.at[core, at_plane(chip, deal_rows)], halo_send.at[k - 1], halo_recv.at[core, chip], region=slot
+        )
+
+    def halo_arrival(which, q):
+        rows = halo.at[which, at_plane(q, deal_rows)]
+        return remote(rows, rows, halo_send.at[0], halo_recv.at[which, q], region=twin)
+
+    def end_halo(which):
         for k in (1, 3, 2):
-            slot = 2 * lax.rem(chip + chips - k, chips) + core
-            halo_copy(which, msg, 0, slot, twin).wait_recv()
-            halo_copy(which, msg, 3 + k, slot, twin).start()
-
-    def end_halo(which, msg):
-        for k in range(4):
-            slot = 2 * lax.rem(chip + k, chips) + 1 - core
-            halo_copy(which, msg, 0, slot, twin).wait_recv()
-
-    start_halo(0, g_msg)
-    g_msg[8] = jnp.zeros(g_msg.shape[1:], bf16)
-    a_msg[8] = jnp.zeros(a_msg.shape[1:], bf16)
+            halo_arrival(which, lax.rem(chip + k, chips)).wait_recv()
+
+        @pl.when(core != which)
+        def _():
+            halo_arrival(which, chip).wait_recv()
+
+    start_deal(0, g_msg)
+    deal[8] = jnp.zeros(deal.shape[1:], bf16)
+    loads[2].wait()
 
     def act_plane(x, carry):
         rows = at_plane(x, PLANE)
@@ -345,11 +411,35 @@
         slope_s[rows, :] = kept * (slope * (1.0 + pre * (1.0 - slope))) * gain[...]
         rinv_s[rows, :] = jnp.broadcast_to(rinv, normed.shape)
         a_stack[x, 0:PLANE, :] = act
-        a_msg[me, at_plane(x, EDGE_ROWS), :] = jnp.dot(extract[...], act, preferred_element_type=f32).astype(bf16)
+        a_msg[at_plane(x, EDGE_ROWS), :] = jnp.dot(extract[...], act, preferred_element_type=f32).astype(bf16)
         return carry
 
     lax.fori_loop(0, BS, act_plane, 0, unroll=2)
-    start_halo(1, a_msg)
+    start_deal(1, a_msg)
+    loads[3].wait()
+    for k in range(1, 8):
+        deal_arrival(lax.rem(me + k, 8)).wait_recv()
+
+    def pick_for(slot):
+        ym, yp, zn, ymz, ypz, bz = neighbours(slot)
+        picked = []
+        for p in range(GROUP):
+            first = p * EDGE_ROWS
+            low, high = slice(first, first + 16), slice(first + 32, first + 48)
+            rows = jnp.concatenate(
+                [deal[ym, high, :], deal[yp, low, :], deal[zn, first : first + EDGE_ROWS, :], deal[ymz, high, :], deal[ypz, low, :]],
+                axis=0,
+            )
+            picked.append(jnp.dot(compact[bz], rows, preferred_element_type=f32).astype(bf16))
+        return jnp.concatenate(picked, axis=0)
+
+    for k in (4, 5, 3, 2, 6, 7, 1):
+        slot = lax.rem(me + k, 8)
+        deliver[slot] = pick_for(slot)
+        halo_copy(k).start()
+    halo[core, at_plane(chip, deal_rows), :] = pick_for(me)
+    my_height = neighbours(me)[5]
+    loads[4].wait()
 
     def own_plane(x, carry):
         moved = jnp.dot(own_spread[...], a_stack[x, 0:PLANE, :], preferred_element_type=f32).astype(bf16)
@@ -365,28 +455,22 @@
                 i * turn : (i + 1) * turn, c * 128 : (c + 1) * 128
             ].T
 
-    def widen(msg, stack, wide):
+    def widen(which, stack, wide):
         wide[0] = jnp.zeros(wide.shape[1:], bf16)
         wide[BS + 1] = jnp.zeros(wide.shape[1:], bf16)
 
         def plane(x, carry):
-            low = pl.ds(pl.multiple_of(x * EDGE_ROWS, 16), 16)
-            high = pl.ds(pl.multiple_of(x * EDGE_ROWS + 32, 16), 16)
-            stack[x, PLANE : PLANE + 16, :] = msg[near[0], high, :]
-            stack[x, PLANE + 16 : PLANE + 32, :] = msg[near[1], low, :]
-            stack[x, PLANE + 32 : PLANE + 80, :] = msg[near[2], at_plane(x, EDGE_ROWS), :]
-            stack[x, PLANE + 80 : PLANE + 96, :] = msg[near[3], high, :]
-            stack[x, PLANE + 96 : PLANE + 112, :] = msg[near[4], low, :]
-            moved = jnp.dot(spread[near[5]], stack[x], preferred_element_type=f32).astype(bf16)
+            stack[x, PLANE:STACK, :] = halo[which, at_plane(x, EDGE_ROWS), :]
+            moved = jnp.dot(spread[my_height], stack[x], preferred_element_type=f32).astype(bf16)
             for c in range(3):
                 wide[x + 1, :, c * 128 : (c + 1) * 128] = moved[c * WIDE : (c + 1) * WIDE]
             return carry
 
         lax.fori_loop(0, BS, plane, 0, unroll=2)
 
-    pass_halo(0, g_msg)
-    end_halo(0, g_msg)
-    widen(g_msg, g_stack, g_wide)
+    loads[5].wait()
+    end_halo(0)
+    widen(0, g_stack, g_wide)
 
     def window(a, b):
         return g_wide[1 - a : 1 - a + BS, (1 - b) * ZPAD : (1 - b) * ZPAD + ROWS, 128:256].reshape(BS * ROWS, 128)
@@ -407,7 +491,6 @@
 
     for q in range(chips):
         twin_copy(q).start()
-    pass_halo(1, a_msg)
 
     def z_copy(k):
         target = lax.rem(chip + k, chips)
@@ -454,10 +537,12 @@
             grad_in[rows, :] = (cot[rows, :].astype(f32) + rinv_s[rows, :] * (dnorm - normed * level)).astype(bf16)
         return carry
 
+    loads[6].wait()
+    loads[7].wait()
     lax.fori_loop(0, BS // count, backward_planes, 0)
 
-    end_halo(1, a_msg)
-    widen(a_msg, a_stack, a_wide)
+    end_halo(1)
+    widen(1, a_stack, a_wide)
 
     def z_wait(k):
         z_copy(k).wait_recv()
@@ -512,8 +597,16 @@
     update[...] = result * 0.25
 
     for which, msg in ((0, g_msg), (1, a_msg)):
-        for index in range(7):
-            halo_copy(which, msg, index, me, twin).wait_send()
+        for k in range(1, 4):
+            deal_copy(which, msg, k).wait_send()
+    for which, msg in ((0, g_msg), (1, a_msg)):
+
+        @pl.when(core != which)
+        def _(which=which, msg=msg):
+            deal_copy(which, msg, 0).wait_send()
+
+    for k in range(1, 8):
+        halo_copy(k).wait_send()
     for q in range(chips):
         twin_copy(q).wait_send()
     for k in range(1, 4):
@@ -537,22 +630,13 @@
     squeeze = squeeze.reshape(PLANE, ROWS)
     squeeze = np.concatenate([squeeze, squeeze], axis=1)
     spread = spread.reshape(GZ, 3 * WIDE, STACK)
-    owner = block_owner[0]
-    block = jnp.sum(jnp.where(owner == lax.axis_index("region"), jnp.arange(slots, dtype=jnp.int32), 0))
-    by, bz = block // GZ, block % GZ
-
-    def holder(y, z):
-        inside = (y >= 0) & (y < GY)
-        return jnp.where(inside, owner[jnp.clip(y * GZ + z, 0, slots - 1)], slots)
-
-    near = jnp.stack(
-        [holder(by - 1, bz), holder(by + 1, bz), holder(by, 1 - bz), holder(by - 1, 1 - bz), holder(by + 1, 1 - bz), bz]
-    ).astype(jnp.int32)
     voxels = BS * BS * BS
     mask = jnp.broadcast_to(voxel_mask[0, 0].astype(bf16)[:, None], (voxels, width))
     vmem = pl.BlockSpec(memory_space=pltpu.VMEM)
     share_rows = TAPS * width // slots
     sem = pltpu.SemaphoreType.DMA
+    tables = [jnp.asarray(table, bf16) for table in (extract_table(), compact_table(), own, spread, squeeze)]
+    hbm = [features[0, 0], cotangent[0, 0], conv_weight, *tables]
     out, grad_in, update = pl.pallas_call(
         fused_kernel,
         out_shape=(
@@ -560,11 +644,15 @@
             jax.ShapeDtypeStruct((voxels, width), bf16),
             jax.ShapeDtypeStruct((share_rows, width), f32),
         ),
-        in_specs=[vmem] * 5 + [pl.BlockSpec(memory_space=pltpu.SMEM)] + [vmem] * 4,
+        in_specs=[pl.BlockSpec(memory_space=pltpu.HBM)] * 8 + [vmem, vmem, pl.BlockSpec(memory_space=pltpu.SMEM)],
         out_specs=(vmem, vmem, vmem),
         scratch_shapes=[
-            pltpu.VMEM((slots + 1, BS * EDGE_ROWS, width), bf16),
-            pltpu.VMEM((slots + 1, BS * EDGE_ROWS, width), bf16),
+            *[pltpu.VMEM(table.shape, bf16) for table in hbm],
+            pltpu.VMEM((BS * EDGE_ROWS, width), bf16),
+            pltpu.VMEM((BS * EDGE_ROWS, width), bf16),
+            pltpu.VMEM((slots + 1, GROUP * EDGE_ROWS, width), bf16),
+            pltpu.VMEM((slots, GROUP * EDGE_ROWS, width), bf16),
+            pltpu.VMEM((2, BS * EDGE_ROWS, width), bf16),
             pltpu.VMEM((BS, STACK, width), bf16),
             pltpu.VMEM((BS, STACK, width), bf16),
             pltpu.VMEM((BS + 2, WIDE, 3 * width), bf16),
@@ -582,7 +670,9 @@
             pltpu.VMEM((slots, 8, width), f32),
             pltpu.VMEM((4, share_rows, width), bf16),
             pltpu.VMEM((4, 8, width), f32),
-            sem((2, 7)), sem((2, slots)),
+            sem((8,)),
+            sem((2, 4)), sem((slots,)),
+            sem((7,)), sem((2, slots // 2)),
             sem((slots // 2,)), sem((slots // 2,)),
             sem((3,)), sem((3,)),
             sem((7,)), sem((7,)),
@@ -594,8 +684,7 @@
         ),
         cost_estimate=pl.CostEstimate(flops=5_000_000_000, bytes_accessed=4_000_000, transcendentals=300_000),
     )(
-        features[0, 0], mask, cotangent[0, 0], norm_gain[None, :], conv_weight, near,
-        jnp.asarray(extract_table(), bf16), jnp.asarray(spread, bf16), jnp.asarray(own, bf16), jnp.asarray(squeeze, bf16),
+        *hbm, mask, norm_gain[None, :], block_owner,
     )
     return (out.reshape(features.shape), grad_in.reshape(cotangent.shape), update)
 

time: 71.9 us -> 56.9 us (0.79)
  Pallas kernels: 55.1 us -> 46.7 us
  between operations: 6.51 us -> 0.69 us
  other arithmetic: 2.07 us -> 0.78 us
    pallas_call x1, Pallas kernels: 55.1 us -> 46.7 us  [fused_body(): pl.pallas_call(fused_kernel, out_shape=(jax.ShapeDtypeStruct((voxels, wid...]
    unnamed x17 -> x21, local copies, waits for them, and re-layouts: 5.87 us -> 8.04 us
    dynamic_slice x1 -> x0, local copies, waits for them, and re-layouts: 1.53 us -> none  [holder(): return jnp.where(inside, owner[jnp.clip(y * GZ + z, 0, slots - 1)], slots)]
    reduce_sum x1 -> x0, other arithmetic: 1.35 us -> none  [fused_body(): jnp.sum(jnp.where(owner == lax.axis_index('region'), jnp.arange(slots, dt...]
where the time goes in v2:
time: 56.9 us; the launch traced here: 56.5 us
  Pallas kernels  46.7 us (82%)
  local copies, waits for them, and re-layouts  8.33 us (15%)
  other arithmetic  0.78 us (1%)
  between operations  0.69 us (1%)
    pallas_call x1, Pallas kernels, fused_body(): pl.pallas_call(fused_kernel, out_shape=(jax.ShapeDtypeStruct((voxels, wid...  46.7 us
    unnamed x21, local copies, waits for them, and re-layouts  8.04 us

profile of v2, /device:TPU:0, one launch (start us, length us, event | category | flops | bytes accessed | tf_op | source)
XLA Modules:
  0.0 56.5 jit_solution(13651233408861273810)
XLA Ops:
  0.6 0.0 copy-start
  0.6 0.8 %convert_reduce_fusion = bf16[1728]{0:T(1024)(128)(2,1)S(1)} fusion(s32[1,1,1728]{2,1,0:T(1,128)} %param.12), kind=kLoop, calls=%fused_computation | loop fusion | flops 1728 | bytes 10368 | tf_op jit(solution)/shard_map/convert_element_type | solution.py:634
  1.4 0.0 copy-start.2
  1.4 0.0 copy-start.3
  1.4 0.3 broadcast_in_dim.4.mask
  1.7 0.0 copy-done
  1.7 0.4 copy-done.2
  2.1 0.0 copy-done.3
  2.1 0.0 copy-start.1
  2.1 1.0 %copy-done.1 = bf16[1,1,1728,128]{3,2,1,0:T(8,128)(2,1)S(1)} copy-done((bf16[1,1,1728,128]{3,2,1,0:T(8,128)(2,1)S(1)}, bf16[1,1,1728,128]{3,2,1,0:T(8,128)(2,1)}, u32[]{:S(2)}) %copy-start.1) | copy-done | bytes 442392
  3.1 0.0 copy-start.4
  3.1 1.1 %copy-done.4 = bf16[2,672,192]{2,1,0:T(8,128)(2,1)S(1)} copy-done((bf16[2,672,192]{2,1,0:T(8,128)(2,1)S(1)}, bf16[2,672,192]{2,1,0:T(8,128)(2,1)}, u32[]{:S(2)}) %copy-start.4) | copy-done | bytes 516120
  4.2 0.0 copy-start.5
  4.2 1.0 %copy-done.5 = bf16[576,144]{1,0:T(8,128)(2,1)S(1)} copy-done((bf16[576,144]{1,0:T(8,128)(2,1)S(1)}, bf16[576,144]{1,0:T(8,128)(2,1)}, u32[]{:S(2)}) %copy-start.5) | copy-done | bytes 165912
  5.2 0.0 copy-start.6
  5.2 0.9 %copy-done.6 = bf16[144,384]{1,0:T(8,128)(2,1)S(1)} copy-done((bf16[144,384]{1,0:T(8,128)(2,1)S(1)}, bf16[144,384]{1,0:T(8,128)(2,1)}, u32[]{:S(2)}) %copy-start.6) | copy-done | bytes 110616
  6.1 0.0 copy-start.7
  6.1 0.7 %copy-done.7 = bf16[2,48,112]{2,1,0:T(8,128)(2,1)S(1)} copy-done((bf16[2,48,112]{2,1,0:T(8,128)(2,1)S(1)}, bf16[2,48,112]{2,1,0:T(8,128)(2,1)}, u32[]{:S(2)}) %copy-start.7) | copy-done | bytes 21528
  6.8 0.0 copy-start.8
  6.8 0.7 %copy-done.8 = bf16[48,144]{1,0:T(8,128)(2,1)S(1)} copy-done((bf16[48,144]{1,0:T(8,128)(2,1)S(1)}, bf16[48,144]{1,0:T(8,128)(2,1)}, u32[]{:S(2)}) %copy-start.8) | copy-done | bytes 13848
  7.6 46.7 %shard_map.130 = (bf16[1728,128]{1,0:T(8,128)(2,1)S(1)}, bf16[1728,128]{1,0:T(8,128)(2,1)S(1)}, f32[432,128]{1,0:T(8,128)S(1)}) custom-call(bf16[1728,128]{1,0:T(8,128)(2,1)S(1)} %bitcast.7, bf16[1728,128]{1,0:T(8,128)(2,1)S(1)} %bitcast.8, bf16[27,128,128]{2,1,0:T(8,128)(2,1)} %weight_h.1, bf16[48,144]{1,0:T(8,128)(2,1)S(1)} %copy-done.8, ...), custom_call_target="tpu_custom_call" | custom-call | flops 5000000000 | bytes 4000000 | tf_op jit(solution)/shard_map/pallas_call | solution.py:640
  54.3 0.8 %copy.17 = bf16[1,1,1728,128]{3,2,1,0:T(8,128)(2,1)} copy(bf16[1,1,1728,128]{3,2,1,0:T(8,128)(2,1)S(1)} %bitcast.6) | data formatting | bytes 884736
  55.0 0.8 %copy.18 = bf16[1,1,1728,128]{3,2,1,0:T(8,128)(2,1)} copy(bf16[1,1,1728,128]{3,2,1,0:T(8,128)(2,1)S(1)} %bitcast.5) | data formatting | bytes 884736
  55.8 0.7 %copy.19 = f32[432,128]{1,0:T(8,128)} copy(f32[432,128]{1,0:T(8,128)S(1)} %get-tuple-element.14) | data formatting | bytes 442368
Async XLA Ops:
  0.6 1.1 %copy-start = (bf16[1,1,1728,128]{3,2,1,0:T(8,128)(2,1)S(1)}, bf16[1,1,1728,128]{3,2,1,0:T(8,128)(2,1)}, u32[]{:S(2)}) copy-start(bf16[1,1,1728,128]{3,2,1,0:T(8,128)(2,1)} %param.11) | copy-start | bytes 1327108
  1.4 0.7 %copy-start.2 = (f32[128]{0:T(128)S(1)}, f32[128]{0:T(128)}, u32[]{:S(2)}) copy-start(f32[128]{0:T(128)} %param.14) | copy-start | bytes 1540
  1.4 0.7 %copy-start.3 = (s32[1,8]{1,0:T(1,128)S(1)}, s32[1,8]{1,0:T(1,128)}, u32[]{:S(2)}) copy-start(s32[1,8]{1,0:T(1,128)} %owner.1) | copy-start | bytes 100
  2.1 1.0 %copy-start.1 = (bf16[1,1,1728,128]{3,2,1,0:T(8,128)(2,1)S(1)}, bf16[1,1,1728,128]{3,2,1,0:T(8,128)(2,1)}, u32[]{:S(2)}) copy-start(bf16[1,1,1728,128]{3,2,1,0:T(8,128)(2,1)} %param.13) | copy-start | bytes 1327108
  3.1 1.1 %copy-start.4 = (bf16[2,672,192]{2,1,0:T(8,128)(2,1)S(1)}, bf16[2,672,192]{2,1,0:T(8,128)(2,1)}, u32[]{:S(2)}) copy-start(bf16[2,672,192]{2,1,0:T(8,128)(2,1)} %constant.13.clone.spread_h) | copy-start | bytes 1548292
  4.2 1.0 %copy-start.5 = (bf16[576,144]{1,0:T(8,128)(2,1)S(1)}, bf16[576,144]{1,0:T(8,128)(2,1)}, u32[]{:S(2)}) copy-start(bf16[576,144]{1,0:T(8,128)(2,1)} %constant.12.clone.own_spread_h) | copy-start | bytes 497668
  5.2 0.9 %copy-start.6 = (bf16[144,384]{1,0:T(8,128)(2,1)S(1)}, bf16[144,384]{1,0:T(8,128)(2,1)}, u32[]{:S(2)}) copy-start(bf16[144,384]{1,0:T(8,128)(2,1)} %constant.14.clone.squeeze_h) | copy-start | bytes 331780
  6.1 0.7 %copy-start.7 = (bf16[2,48,112]{2,1,0:T(8,128)(2,1)S(1)}, bf16[2,48,112]{2,1,0:T(8,128)(2,1)}, u32[]{:S(2)}) copy-start(bf16[2,48,112]{2,1,0:T(8,128)(2,1)} %constant.11.clone.compact_h) | copy-start | bytes 64516
  6.8 0.7 %copy-start.8 = (bf16[48,144]{1,0:T(8,128)(2,1)S(1)}, bf16[48,144]{1,0:T(8,128)(2,1)}, u32[]{:S(2)}) copy-start(bf16[48,144]{1,0:T(8,128)(2,1)} %constant.10.clone.extract_h) | copy-start | bytes 41476

commit v3 on v2

--- a/solution.py
+++ b/solution.py
@@ -496,12 +496,12 @@
         target = lax.rem(chip + k, chips)
         return remote(pair16.at[target], from_z.at[k - 1], z_send.at[k - 1], z_recv.at[k - 1], region=2 * target + core)
 
-    for q in range(chips):
-        twin_copy(q).wait_recv()
     for k in (2, 1, 3):
         q = lax.rem(chip + k, chips)
+        twin_copy(q).wait_recv()
         pair16[q] = (part[share_of(2 * q + core), :] + from_twin[q]).astype(bf16)
         z_copy(k).start()
+    twin_copy(chip).wait_recv()
     pair_own[...] = part[share_of(me), :] + from_twin[chip]
 
     count = 3
@@ -680,7 +680,7 @@
             sem((3,)), sem((3,)),
         ],
         compiler_params=pltpu.CompilerParams(
-            collective_id=0, has_side_effects=True, vmem_limit_bytes=50 * 1024 * 1024
+            collective_id=0, has_side_effects=True, vmem_limit_bytes=60 * 1024 * 1024
         ),
         cost_estimate=pl.CostEstimate(flops=5_000_000_000, bytes_accessed=4_000_000, transcendentals=300_000),
     )(

time: 56.9 us -> 52.9 us (0.930)
  local copies, waits for them, and re-layouts: 8.33 us -> 4.7 us
    unnamed x21 -> x7, local copies, waits for them, and re-layouts: 8.04 us -> 3.64 us
    broadcast_in_dim x1, local copies, waits for them, and re-layouts: 0.29 us -> 1.06 us  [fused_body(): jnp.broadcast_to(voxel_mask[0, 0].astype(bf16)[:, None], (voxels, width))]
where the time goes in v3:
time: 52.9 us; the launch traced here: 52.7 us
  Pallas kernels  46.6 us (88%)
  local copies, waits for them, and re-layouts  4.7 us (9%)
  other arithmetic  0.72 us (1%)
  between operations  0.65 us (1%)
    pallas_call x1, Pallas kernels, fused_body(): pl.pallas_call(fused_kernel, out_shape=(jax.ShapeDtypeStruct((voxels, wid...  46.6 us
    unnamed x7, local copies, waits for them, and re-layouts  3.64 us
    broadcast_in_dim x1, local copies, waits for them, and re-layouts, fused_body(): jnp.broadcast_to(voxel_mask[0, 0].astype(bf16)[:, None], (voxels, width))  1.06 us

profile of v3, /device:TPU:0, one launch (start us, length us, event | category | flops | bytes accessed | tf_op | source)
XLA Modules:
  0.0 52.7 jit_solution(16656798643791393523)
XLA Ops:
  0.6 0.7 %convert_reduce_fusion = bf16[1728]{0:T(1024)(128)(2,1)S(1)} fusion(s32[1,1,1728]{2,1,0:T(1,128)} %param.12), kind=kLoop, calls=%fused_computation | loop fusion | flops 1728 | bytes 10368 | tf_op jit(solution)/shard_map/convert_element_type | solution.py:634
  1.4 1.1 %broadcast_in_dim.4.mask = bf16[1728,128]{1,0:T(8,128)(2,1)} broadcast(bf16[1728]{0:T(1024)(128)(2,1)S(1)} %convert_reduce_fusion), dimensions={0} | broadcast | bytes 445824 | tf_op jit(solution)/shard_map/broadcast_in_dim | solution.py:634
  2.4 46.6 %shard_map.130 = (bf16[1728,128]{1,0:T(8,128)(2,1)}, bf16[1728,128]{1,0:T(8,128)(2,1)}, f32[432,128]{1,0:T(8,128)}) custom-call(bf16[1728,128]{1,0:T(8,128)(2,1)} %bitcast.7, bf16[1728,128]{1,0:T(8,128)(2,1)} %bitcast.8, bf16[27,128,128]{2,1,0:T(8,128)(2,1)} %weight_h.1, bf16[48,144]{1,0:T(8,128)(2,1)} %constant.10.clone.extract_h, ...), custom_call_target="tpu_custom_call" | custom-call | flops 5000000000 | bytes 4000000 | tf_op jit(solution)/shard_map/pallas_call | solution.py:640
  49.0 0.0 copy-start
  49.0 1.9 %copy.17 = bf16[1,1,1728,128]{3,2,1,0:T(8,128)(2,1)} copy(bf16[1,1,1728,128]{3,2,1,0:T(8,128)(2,1)} %bitcast.6) | data formatting | bytes 884736
  50.9 0.0 copy-done
  50.9 0.0 copy-start.1
  50.9 0.8 %copy.18 = bf16[1,1,1728,128]{3,2,1,0:T(8,128)(2,1)} copy(bf16[1,1,1728,128]{3,2,1,0:T(8,128)(2,1)S(1)} %bitcast.5) | data formatting | bytes 884736
  51.7 0.3 copy-done.1
  52.0 0.7 %copy.19 = f32[432,128]{1,0:T(8,128)} copy(f32[432,128]{1,0:T(8,128)S(1)} %copy-done.1) | data formatting | bytes 442368
Async XLA Ops:
  49.0 1.9 %copy-start = (bf16[1728,128]{1,0:T(8,128)(2,1)S(1)}, bf16[1728,128]{1,0:T(8,128)(2,1)}, u32[]{:S(2)}) copy-start(bf16[1728,128]{1,0:T(8,128)(2,1)} %get-tuple-element.7) | copy-start | bytes 1327108
  50.9 1.1 %copy-start.1 = (f32[432,128]{1,0:T(8,128)S(1)}, f32[432,128]{1,0:T(8,128)}, u32[]{:S(2)}) copy-start(f32[432,128]{1,0:T(8,128)} %get-tuple-element.14) | copy-start | bytes 663556
